TPU v7x, 32 devices: a whole 2x2x4 slice. The times are simulated.
32 devices in a mesh: dp: 4 (over y, x), entity: 8 (over z, core).
Axes of the slice: x: 2, y: 2, z: 4, core: 2. Of those that a mesh axis runs over, the one named last changes fastest.
Arguments:
- entities: float32 [8, 4096, 256], P('entity'), may hold values from -20 to 20
- relations: float32 [256, 256, 256], P('entity'), may hold values from -0.375 to 0.375
- candidate_blocks: int32 [32, 8], P('dp'), may hold values from 0 to 7, as said below
- list_lengths: int32 [4, 8], P('dp'), may hold values from 2 to 8, as said below
- head_offsets: int32 [4096], P(('dp', 'entity')), may hold values from 0 to 4095
- relation_offsets: int32 [4096], P(('dp', 'entity')), may hold values from 0 to 31
- target_codes: int32 [4096], P(('dp', 'entity')), may hold values from 0 to 32767
Outputs:
- loss: float32 [4096], P(('dp', 'entity'))
- entity_grad: float32 [8, 4096, 256], P('entity', 'dp')
Inputs may be any that keep to these rules, and one draw needn't show every extreme that they name: `candidate_blocks`: each row names 8 different blocks. Among the entries of the 8 rows of one dp group, used or not, no block is named more than 8 times; in every dp group one block is named exactly 8 times, each time at a used entry. `list_lengths`: the 8 lengths of one dp group sum to 40, and one of them is 8.
All inputs are finite; a program needn't handle non-finite values.
Results may differ from a plain program's by a relative error of at most 0.0025.
The roundings to bfloat16 on the way count: a program that leaves them out, or rounds other values in their place, can miss the bound.
Values may be sent and summed in bfloat16 or wider, within the bound.
A program may use at most 64 MiB of HBM per device.

v0:
```python
import jax
import jax.numpy as jnp
from jax import lax
from jax.sharding import PartitionSpec as P

CAP = 12


negative_floor = -1e30
slots_per_step = 4


def score_rows(queries, row_block):
    return lax.dot_general(
        queries, row_block, (((1,), (1,)), ((), ())), preferred_element_type=jnp.float32
    )


def step_view(values, slot_count):
    return values.reshape(
        (slot_count // slots_per_step, slots_per_step * values.shape[1]) + values.shape[2:]
    )


def slot_stats(row_block, queries, targets, in_use):
    slot_count, trip_count = targets.shape
    active = jnp.broadcast_to(in_use[:, None], (slot_count, trip_count))
    positions = jnp.arange(row_block.shape[0], dtype=jnp.int32)

    def one_step(inputs):
        step_queries, step_targets = inputs
        scores = score_rows(step_queries, row_block)
        maxima = jnp.max(scores, axis=1)
        masses = jnp.sum(jnp.exp(scores - maxima[:, None]), axis=1)
        is_target = positions[None, :] == step_targets[:, None]
        picked = jnp.sum(jnp.where(is_target, scores, 0.0), axis=1)
        return (maxima, masses, picked)

    maxima, masses, picked = lax.map(
        one_step, (step_view(queries, slot_count), step_view(targets, slot_count))
    )
    maxima = jnp.where(active, maxima.reshape(slot_count, trip_count), negative_floor)
    masses = jnp.where(active, masses.reshape(slot_count, trip_count), 0.0)
    picked = jnp.where(active, picked.reshape(slot_count, trip_count), 0.0)
    return (maxima, masses, picked)


def slot_grads(row_block, queries, targets, in_use, slot_norms):
    slot_count, trip_count = targets.shape
    active = jnp.broadcast_to(in_use[:, None], (slot_count, trip_count))
    positions = jnp.arange(row_block.shape[0], dtype=jnp.int32)

    def one_step(carry, inputs):
        step_queries, step_targets, step_norms, step_active = inputs
        scores = score_rows(step_queries, row_block)
        weights = jnp.exp(scores - step_norms[:, None])
        is_target = (positions[None, :] == step_targets[:, None]).astype(jnp.float32)
        coefficients = jnp.where(step_active[:, None], weights - is_target, 0.0).astype(
            jnp.bfloat16
        )
        update = lax.dot_general(
            coefficients, step_queries, (((0,), (0,)), ((), ())), preferred_element_type=jnp.float32
        )
        return (carry + update, None)

    initial = jnp.zeros((row_block.shape[0], queries.shape[2]), jnp.float32)
    inputs = (
        step_view(queries, slot_count),
        step_view(targets, slot_count),
        step_view(slot_norms, slot_count),
        step_view(active, slot_count),
    )
    result, unused = lax.scan(one_step, initial, inputs)
    return result


def per_device(
    entities,
    relations,
    candidate_blocks,
    list_lengths,
    head_offsets,
    relation_offsets,
    target_codes,
):
    entity_count = lax.axis_size("entity")
    owner = lax.axis_index("entity")
    table = entities[0]
    block_rows = table.shape[0]
    local_relations = relations.shape[0]
    head_rows = jnp.take(table, head_offsets, axis=0)
    products = jnp.einsum("td,rde->tre", head_rows, relations, precision=lax.Precision.HIGHEST)
    selector = (
        relation_offsets[:, None] == jnp.arange(local_relations, dtype=jnp.int32)[None, :]
    ).astype(jnp.float32)
    query = jnp.sum(products * selector[:, :, None], axis=1).astype(jnp.bfloat16)
    gathered, all_codes = (
        lax.all_gather(query[None], "entity", axis=0, tiled=True),
        lax.all_gather(target_codes[None], "entity", axis=0, tiled=True),
    )
    lengths = list_lengths[0]
    entry_index = jnp.arange(candidate_blocks.shape[1], dtype=jnp.int32)
    counted = entry_index[None, :] < lengths[:, None]
    listed = jnp.any(counted & (candidate_blocks == owner), axis=1)
    ranking = jnp.cumsum(listed.astype(jnp.int32)) - 1
    capacity = min(CAP, entity_count)
    slot_index = jnp.arange(capacity, dtype=jnp.int32)
    set_numbers = jnp.arange(entity_count, dtype=jnp.int32)
    matches = listed[None, :] & (ranking[None, :] == slot_index[:, None])
    slot_set = jnp.sum(jnp.where(matches, set_numbers[None, :], 0), axis=1)
    slot_used = jnp.any(matches, axis=1)
    slot_queries = jnp.take(gathered, slot_set, axis=0)
    slot_codes = jnp.take(all_codes, slot_set, axis=0)
    slot_lists = jnp.take(candidate_blocks, slot_set, axis=0)
    slot_lengths = jnp.take(lengths, slot_set)
    chosen = slot_codes // block_rows % slot_lengths[:, None]
    target_block = jnp.sum(
        jnp.where(chosen[:, :, None] == entry_index[None, None, :], slot_lists[:, None, :], 0),
        axis=2,
    )
    slot_targets = jnp.where(target_block == owner, slot_codes % block_rows, -1)
    rounded_table = table.astype(jnp.bfloat16)
    maxima, masses, picked = slot_stats(rounded_table, slot_queries, slot_targets, slot_used)
    safe_rank = jnp.clip(ranking, 0, capacity - 1)
    set_max = jnp.where(listed[:, None], jnp.take(maxima, safe_rank, axis=0), negative_floor)
    set_mass = jnp.where(listed[:, None], jnp.take(masses, safe_rank, axis=0), 0.0)
    set_target = jnp.where(listed[:, None], jnp.take(picked, safe_rank, axis=0), 0.0)
    top_max = lax.pmax(set_max.astype(jnp.bfloat16), "entity").astype(set_max.dtype)
    scaled_mass = set_mass * jnp.exp(set_max - top_max)
    top_mass, top_target = lax.psum((scaled_mass, set_target), "entity")
    log_norm = top_max + jnp.log(top_mass)
    loss = lax.dynamic_index_in_dim(log_norm - top_target, owner, 0, keepdims=False)
    slot_norms = jnp.take(log_norm, slot_set, axis=0)
    gradient = lax.psum_scatter(
        slot_grads(rounded_table, slot_queries, slot_targets, slot_used, slot_norms),
        "dp",
        scatter_dimension=0,
        tiled=True,
    )
    return (loss, gradient[None])


def solution(mesh):
    return jax.shard_map(
        per_device,
        mesh=mesh,
        in_specs=(
            P("entity", None, None),
            P("entity", None, None),
            P("dp", None),
            P("dp", None),
            P(("dp", "entity")),
            P(("dp", "entity")),
            P(("dp", "entity")),
        ),
        out_specs=(P(("dp", "entity")), P("entity", "dp", None)),
        check_vma=False,
    )
```

profile of v0, /device:TPU:0, one launch (start us, length us, event | category | flops | bytes accessed | tf_op | source)
XLA Modules:
  0.0 169.2 jit_solution(18018036720354445324)
XLA Ops:
  7.2 0.9 fusion.27
  8.4 1.3 gather_fusion.3
  9.7 1.2 gather_fusion.4
  11.1 0.7 compare_select_fusion.7
  11.7 0.7 compare_and_fusion.2
  12.5 13.5 %all-gather.2 = s32[8,1,128]{2,1,0:T(1,128)S(1)} all-gather(s32[1,1,128]{2,1,0:T(1,128)} %bitcast.92), channel_id=3, replica_groups=mesh['dp'=4,'entity'=8] {'entity'}, dimensions={0}, use_global_device_ids=true | all-gather | bytes 4608 | tf_op jit(solution)/shard_map/all_gather | solution.py:99
  27.1 0.7 fusion.19
  27.8 2.4 %bitcast_convert_fusion = bf16[4096,256]{1,0:T(8,128)(2,1)S(1)} fusion(f32[1,4096,256]{2,1,0:T(8,128)} %param.13), kind=kLoop, calls=%fused_computation.97 | loop fusion | flops 1048576 | bytes 6291456 | tf_op jit(solution)/shard_map/convert_element_type | solution.py:122
  30.2 2.9 %gather_fusion = f32[128,256]{1,0:T(8,128)S(1)} fusion(f32[4096,256]{1,0:T(8,128)} %bitcast.80, s32[1024]{0:T(1024)S(1)} %pad_clamp_fusion.3), kind=kCustom, calls=%fused_computation.4 | custom fusion | bytes 262656 | tf_op jit(solution)/shard_map/jit(_take)/gather | solution.py:91
  33.1 8.7 %multiply_reduce_fusion = bf16[128,256]{1,0:T(8,128)(2,1)S(1)} fusion(f32[32,256,256]{2,1,0:T(8,128)} %param.14, f32[128,32]{0,1:T(8,128)S(1)} %fusion.19, f32[128,256]{1,0:T(8,128)S(1)} %gather_fusion, pred[128]{0:T(512)(128)(4,1)S(1)} %compare_and_fusion.2), kind=kOutput, calls=%fused_computation.29 | convolution fusion | flops 3223322624 | bytes 8601728 | tf_op jit(solution)/shard_map/td,rde->tre/dot_general | solution.py:92
  41.9 14.9 %all-gather = bf16[1024,256]{1,0:T(8,128)(2,1)S(1)} all-gather(bf16[128,256]{1,0:T(8,128)(2,1)S(1)} %multiply_reduce_fusion), channel_id=2, replica_groups=mesh['dp'=4,'entity'=8] {'entity'}, dimensions={0}, use_global_device_ids=true | all-gather | bytes 589824 | tf_op jit(solution)/shard_map/all_gather | solution.py:98
  56.8 0.6 gather_fusion.1
  57.6 8.7 %while.26 = (s32[]{:T(128)}, f32[2,512]{1,0:T(2,128)S(1)}, f32[2,512]{1,0:T(2,128)S(1)}, f32[2,512]{1,0:T(2,128)S(1)}, bf16[2,512,256]{2,1,0:T(8,128)(2,1)S(1)},...) while((s32[]{:T(128)}, f32[2,512]{1,0:T(2,128)S(1)}, ...), condition=%wide.region_10.11_spmd.clone, body=%wide.region_6.10_spmd.clone.sunk | while | flops 1086323200 | bytes 19163248 | solution.py:39
  57.6 1.4 fusion.45
  59.0 2.8 %select_reduce_fusion.4 = (f32[512]{0:T(512)S(1)}, f32[512]{0:T(512)S(1)}) fusion(f32[512,4096]{1,0:T(8,128)S(1)} %get-tuple-element.265, s32[512]{0:T(512)S(1)} %bitcast.87, f32[512]{0:T(512)S(1)} %get-tuple-element.264), kind=kLoop, calls=%fused_computation.12.clone.1 | loop fusion | flops 10484736 | bytes 8396800 | tf_op jit(solution)/shard_map/while/body/eval_jaxpr/reduce_sum | solution.py:36
  62.0 1.4 fusion.45
  63.4 2.8 %select_reduce_fusion.4 = (f32[512]{0:T(512)S(1)}, f32[512]{0:T(512)S(1)}) fusion(f32[512,4096]{1,0:T(8,128)S(1)} %get-tuple-element.265, s32[512]{0:T(512)S(1)} %bitcast.87, f32[512]{0:T(512)S(1)} %get-tuple-element.264), kind=kLoop, calls=%fused_computation.12.clone.1 | loop fusion | flops 10484736 | bytes 8396800 | tf_op jit(solution)/shard_map/while/body/eval_jaxpr/reduce_sum | solution.py:36
  67.2 13.9 %pmax.7 = bf16[8,128]{1,0:T(8,128)(2,1)S(1)} all-reduce(bf16[8,128]{1,0:T(8,128)(2,1)S(1)} %fusion.31), channel_id=1, replica_groups=mesh['dp'=4,'entity'=8] {'entity'}, use_global_device_ids=true, to_apply=%region_11.13 | all-reduce | flops 1024 | bytes 4096 | tf_op jit(solution)/shard_map/pmax | solution.py:128
  81.6 0.6 gather_fusion.7
  82.3 14.1 %all-reduce = (f32[8,128]{1,0:T(8,128)S(1)}, f32[8,128]{1,0:T(8,128)S(1)}) all-reduce(f32[8,128]{1,0:T(8,128)S(1)} %get-tuple-element.177, f32[8,128]{1,0:T(8,128)S(1)} %get-tuple-element.176), channel_id=1, replica_groups=mesh['dp'=4,'entity'=8] {'entity'}, use_global_device_ids=true, to_apply=%region_12.14 | all-reduce | flops 2048 | bytes 16384 | tf_op jit(solution)/shard_map/psum | solution.py:130
  97.1 14.1 %while.27 = (s32[]{:T(128)}, f32[4096,256]{1,0:T(8,128)}, pred[2,512]{1,0:T(4,128)(4,1)S(1)}, bf16[2,512,256]{2,1,0:T(8,128)(2,1)S(1)}, bf16[4096,256]{1,0:T(8,1...) while((s32[]{:T(128)}, f32[4096,256]{1,0:T(8,128)}, ...), condition=%wide.region_15.17_spmd.clone, body=%wide.region_14.16_spmd.clone.sunk | while | flops 2162163712 | bytes 11025011 | solution.py:73
  97.2 5.9 %convolution_add_fusion.2 = f32[4096,256]{1,0:T(8,128)} fusion(f32[4096,256]{1,0:T(8,128)} %get-tuple-element.312, pred[]{:T(512)S(6)} %compare.11, bf16[4096,256]{1,0:T(8,128)(2,1)S(1)} %get-tuple-element.324, s32[512]{0:T(512)S(1)} %bitcast.89, f32[512]{0:T(512)S(1)} %bitcast.90, pred[512]{0:T(512)(128)(4,1)S(1)} %dynamic-slice_reduce_fusion.2, ...), kind=kOutput, calls=%fused_computation.21.clone.1 | convolution fusion | flops 2162163712 | bytes 11015681 | tf_op jit(solution)/shard_map/while/body/eval_jaxpr/dot_general | solution.py:61
  103.2 8.1 %convolution_add_fusion.2 = f32[4096,256]{1,0:T(8,128)} fusion(f32[4096,256]{1,0:T(8,128)} %get-tuple-element.312, pred[]{:T(512)S(6)} %compare.11, bf16[4096,256]{1,0:T(8,128)(2,1)S(1)} %get-tuple-element.324, s32[512]{0:T(512)S(1)} %bitcast.89, f32[512]{0:T(512)S(1)} %bitcast.90, pred[512]{0:T(512)(128)(4,1)S(1)} %dynamic-slice_reduce_fusion.2, ...), kind=kOutput, calls=%fused_computation.21.clone.1 | convolution fusion | flops 2162163712 | bytes 11015681 | tf_op jit(solution)/shard_map/while/body/eval_jaxpr/dot_general | solution.py:61
  111.8 50.6 %reduce-scatter.2.cloned.1.call-done = f32[1024,256]{1,0:T(8,128)} async-done(((f32[4096,256]{1,0:T(8,128)}), f32[1024,256]{1,0:T(8,128)}) %reduce-scatter.2.cloned.1.call-update) | async-done | bytes 1048592 | tf_op jit(solution)/shard_map/reduce_scatter | solution.py:134
  (62 shorter events, 4.9 us)
Async XLA Ops:
  7.2 155.2 %reduce-scatter.2.cloned.1.call-start = ((), (), s32[]{:S(2)}) async-start(), calls=%async_computation.1 | async-start | bytes 5242880 | tf_op jit(solution)/shard_map/reduce_scatter | solution.py:134
Sparse Core Ops, SparseCore 0:
  111.4 50.9 reduce-scatter.1
where the time goes:
time: 170 us; the launch traced here: 169 us
  blocking collectives  56.4 us (33%)
  waiting for transfers between devices  50.6 us (30%)
  matrix products  25.5 us (15%)
  between operations  14.2 us (8%)
  other arithmetic  12.3 us (7%)
  local copies, waits for them, and re-layouts  10.1 us (6%)
    reduce_scatter x1, waiting for transfers between devices, per_device(): lax.psum_scatter(slot_grads(rounded_table, slot_queries, slot_targets, sl...  50.6 us
    all_gather x1, blocking collectives, per_device(): lax.all_gather(query[None], 'entity', axis=0, tiled=True)  14.9 us
    psum x1, blocking collectives, per_device(): top_mass, top_target = lax.psum((scaled_mass, set_target), 'entity')  14.1 us
    dot_general x2, matrix products, one_step(): lax.dot_general(coefficients, step_queries, (((0,), (0,)), ((), ())), pre...  14 us
    pmax x1, blocking collectives, per_device(): lax.pmax(set_max.astype(jnp.bfloat16), 'entity').astype(set_max.dtype)  13.9 us
    all_gather x1, blocking collectives, per_device(): lax.all_gather(target_codes[None], 'entity', axis=0, tiled=True)  13.5 us
    dot_general x1, matrix products, per_device(): jnp.einsum('td,rde->tre', head_rows, relations, precision=lax.Precision.H...  8.74 us
    reduce_sum x2, other arithmetic, one_step(): picked = jnp.sum(jnp.where(is_target, scores, 0.0), axis=1)  5.63 us
  transfers between devices with their start and end apart: 1, of which 1 were waited for; matrix products, arithmetic and copies ran while one was open for 0% of the time, Pallas kernels for 0%

commit v1 on v0

--- a/solution.py
+++ b/solution.py
@@ -1,6 +1,8 @@
 import jax
 import jax.numpy as jnp
 from jax import lax
+from jax.experimental import pallas as pl
+from jax.experimental.pallas import tpu as pltpu
 from jax.sharding import PartitionSpec as P
 
 CAP = 12
@@ -140,9 +142,425 @@
     return (loss, gradient[None])
 
 
+LOADS = 4
+META = 16
+LAG = 2
+PAIRS = 16
+TILE = 256
+
+
+def split3(value):
+    first = value.astype(jnp.bfloat16)
+    rest = value - first.astype(jnp.float32)
+    second = rest.astype(jnp.bfloat16)
+    third = (rest - second.astype(jnp.float32)).astype(jnp.bfloat16)
+    return first, second, third
+
+
+def fused_kernel(
+    lists_ref,
+    lengths_ref,
+    heads_ref,
+    kinds_ref,
+    codes_ref,
+    table_hbm,
+    relations_hbm,
+    loss_ref,
+    grad_ref,
+    table,
+    operators,
+    keys,
+    head_rows,
+    kind_rows,
+    product,
+    chunks,
+    masses,
+    maxima,
+    stats,
+    from_sibling,
+    from_z,
+    from_plane,
+    load_sem,
+    z_send,
+    z_recv,
+    x_send,
+    x_recv,
+    y_send,
+    y_recv,
+    xd_send,
+    xd_recv,
+    yd_send,
+    yd_recv,
+    s_send,
+    s_recv,
+    stat_send,
+    stat_recv,
+):
+    a = lax.axis_index("dp")
+    e = lax.axis_index("entity")
+    z, c = e // 2, e % 2
+    block_rows, width = table.shape
+    share = keys.shape[0]
+    trips = codes_ref.shape[1]
+    chunk_rows = trips + META
+    first_rows = 80
+    kinds = operators.shape[0]
+
+    def group(g):
+        return ((a // 2 + g // 2) % 2) * 2 + (a % 2 + g % 2) % 2
+
+    def chunk_of(g, j, core):
+        return group(g) * 8 + ((z + 4 - j) % 4) * 2 + core
+
+    sibling = (a, z * 2 + 1 - c)
+    plane = [(group(g), e) for g in (1, 2, 3)]
+    along_z = [(a, ((z + j) % 4) * 2 + c) for j in (1, 2, 3)]
+    x_device, y_device = plane[0], plane[1]
+
+    def remote(source, target, send_sem, recv_sem, device):
+        return pltpu.make_async_remote_copy(
+            src_ref=source,
+            dst_ref=target,
+            send_sem=send_sem,
+            recv_sem=recv_sem,
+            device_id=device,
+            device_id_type=pl.DeviceIdType.MESH,
+        )
+
+    barrier = pltpu.get_barrier_semaphore()
+    for device in [sibling] + plane + along_z:
+        pl.semaphore_signal(barrier, inc=1, device_id=device, device_id_type=pl.DeviceIdType.MESH)
+
+    table_load = pltpu.make_async_copy(table_hbm.at[0], table, load_sem.at[LOADS])
+    table_load.start()
+    per_load = kinds // LOADS
+    loads = []
+    for n in range(LOADS):
+        span = pl.ds(n * per_load, per_load)
+        load = pltpu.make_async_copy(relations_hbm.at[span], operators.at[span], load_sem.at[n])
+        load.start()
+        loads.append(load)
+
+    length = lengths_ref[0, e]
+    codes = codes_ref[...]
+    entry = codes // block_rows
+    wraps = jnp.zeros_like(entry)
+    for n in range(1, 4):
+        wraps = wraps + jnp.where(entry >= n * length, 1, 0)
+    pick = entry - wraps * length
+    row_index = lax.broadcasted_iota(jnp.int32, (META, trips), 0)
+    target_block = jnp.zeros_like(entry)
+    used = jnp.zeros((META, trips), jnp.float32)
+    for k in range(lists_ref.shape[1]):
+        named = lists_ref[e, k]
+        target_block = target_block + jnp.where(pick == k, named, 0)
+        counted = jnp.where(k < length, named, -9)
+        used = used + jnp.where(row_index - 2 == counted, 1.0, 0.0)
+    target_id = target_block * block_rows + codes % block_rows
+    high = (target_id // 256).astype(jnp.float32)
+    low = (target_id % 256).astype(jnp.float32)
+    notes = jnp.where(row_index == 0, high, jnp.where(row_index == 1, low, used))
+
+    table_load.wait()
+
+    def fetch(n, unused):
+        head_rows[pl.ds(n, 1), :] = table[pl.ds(heads_ref[n], 1), :]
+        kind_rows[pl.ds(n, 1), :] = jnp.full((1, width), kinds_ref[n], jnp.int32)
+        return unused
+
+    lax.fori_loop(0, trips, fetch, 0, unroll=8)
+    parts = jnp.concatenate(split3(head_rows[...]), axis=0)
+
+    def one_kind(r, unused):
+        r1, r2, r3 = split3(operators[r])
+        p1 = jnp.dot(parts, r1, preferred_element_type=jnp.float32)
+        p2 = jnp.dot(parts[: 2 * trips], r2, preferred_element_type=jnp.float32)
+        p3 = jnp.dot(parts[:trips], r3, preferred_element_type=jnp.float32)
+        small = (p1[2 * trips :] + p2[trips:]) + p3
+        total = p1[:trips] + ((p1[trips : 2 * trips] + p2[:trips]) + small)
+        product[...] = jnp.where(kind_rows[...] == r, total, product[...])
+        return unused
+
+    product[...] = jnp.zeros_like(product)
+    for n in range(LOADS):
+        loads[n].wait()
+        lax.fori_loop(n * per_load, (n + 1) * per_load, one_kind, 0, unroll=2)
+
+    mine = chunk_of(0, 0, c)
+    chunks[mine, 0:trips, :] = product[...].astype(jnp.bfloat16)
+    chunks[mine, trips:chunk_rows, :] = jnp.concatenate(
+        [notes, jnp.zeros_like(notes)], axis=1
+    ).astype(jnp.bfloat16)
+
+    pl.semaphore_wait(barrier, 7)
+
+    def z_copy(j, slot):
+        return remote(
+            chunks.at[slot], chunks.at[slot], z_send.at[j - 1], z_recv.at[j - 1], along_z[j - 1]
+        )
+
+    for j in (1, 2, 3):
+        z_copy(j, mine).start()
+
+    keys[...] = table[pl.ds(pl.multiple_of(a * share, share), share), :].astype(jnp.bfloat16)
+
+    def x_copy(j, slot):
+        return remote(chunks.at[slot], chunks.at[slot], x_send.at[j], x_recv.at[j], x_device)
+
+    def y_copy(j, slot):
+        return remote(chunks.at[slot], chunks.at[slot], y_send.at[j], y_recv.at[j], y_device)
+
+    def yd_copy(j, slot):
+        part = chunks.at[slot, pl.ds(0, first_rows)]
+        return remote(part, part, yd_send.at[j], yd_recv.at[j], y_device)
+
+    def xd_copy(j, slot):
+        part = chunks.at[slot, pl.ds(first_rows, chunk_rows - first_rows)]
+        return remote(part, part, xd_send.at[j], xd_recv.at[j], x_device)
+
+    def s_copy(i, slot):
+        return remote(chunks.at[slot], chunks.at[slot], s_send.at[i], s_recv.at[i], sibling)
+
+    def pair_of(i):
+        return group(i % 4) * 4 + (z + 4 - i // 4) % 4
+
+    def read_notes(pair):
+        sheet = jnp.concatenate(
+            [chunks[pair * 2 + n, trips:chunk_rows, 0:trips] for n in range(2)], axis=1
+        ).astype(jnp.float32)
+        rows = lax.broadcasted_iota(jnp.int32, sheet.shape, 0)
+        in_use = jnp.sum(jnp.where(rows == 2 + e, sheet, 0.0), axis=0, keepdims=True) > 0.0
+        target = (sheet[0:1] * 256.0 + sheet[1:2]).astype(jnp.int32)
+        return in_use, target - (e * block_rows + a * share)
+
+    def pair_queries(pair):
+        return jnp.concatenate([chunks[pair * 2 + n, 0:trips, :] for n in range(2)], axis=0)
+
+    row_iota = lax.broadcasted_iota(jnp.int32, (TILE, 2 * trips), 0)
+
+    def fold(value, op):
+        return op(value.reshape(TILE // 8, 8, 2 * trips), axis=0)
+
+    def pair_stats(pair):
+        queries = pair_queries(pair)
+        in_use, target = read_notes(pair)
+        top = None
+        for n in range(share // TILE):
+            scores = lax.dot_general(
+                keys[n * TILE : (n + 1) * TILE, :],
+                queries,
+                (((1,), (1,)), ((), ())),
+                preferred_element_type=jnp.float32,
+            )
+            masses[pair, n * TILE : (n + 1) * TILE, :] = scores
+            tile_top = fold(scores, jnp.max)
+            top = tile_top if top is None else jnp.maximum(top, tile_top)
+        top = jnp.max(top, axis=0, keepdims=True)
+        total = jnp.zeros((8, 2 * trips), jnp.float32)
+        picked = jnp.zeros((8, 2 * trips), jnp.float32)
+        for n in range(share // TILE):
+            scores = masses[pair, n * TILE : (n + 1) * TILE, :]
+            mass = jnp.exp(scores - top)
+            masses[pair, n * TILE : (n + 1) * TILE, :] = mass
+            total = total + fold(mass, jnp.sum)
+            picked = picked + fold(jnp.where(row_iota == target - n * TILE, scores, 0.0), jnp.sum)
+        total = jnp.sum(total, axis=0, keepdims=True)
+        maxima[pl.ds(pair, 1), :] = top
+        stats[0, 0, pl.ds(pair, 1), :] = jnp.where(in_use, top + jnp.log(total), negative_floor)
+        stats[0, 1, pl.ds(pair, 1), :] = jnp.sum(picked, axis=0, keepdims=True)
+
+    def gather_step(i, unused):
+        j, g = i // 4, i % 4
+
+        @pl.when(i < PAIRS)
+        def _():
+            slot = chunk_of(g, j, c)
+
+            @pl.when(g == 0)
+            def _():
+                for k in (1, 2, 3):
+
+                    @pl.when(j == k)
+                    def _():
+                        z_copy(k, slot).wait_recv()
+
+                x_copy(j, slot).start()
+                y_copy(j, slot).start()
+
+            @pl.when(g == 1)
+            def _():
+                x_copy(j, slot).wait_recv()
+                yd_copy(j, slot).start()
+
+            @pl.when(g == 2)
+            def _():
+                y_copy(j, slot).wait_recv()
+                xd_copy(j, slot).start()
+
+            @pl.when(g == 3)
+            def _():
+                yd_copy(j, slot).wait_recv()
+                xd_copy(j, slot).wait_recv()
+
+            s_copy(i, slot).start()
+
+        @pl.when(i >= LAG)
+        def _():
+            k = i - LAG
+            s_copy(k, chunk_of(k % 4, k // 4, 1 - c)).wait_recv()
+            pair_stats(pair_of(k))
+
+        return unused
+
+    lax.fori_loop(0, PAIRS + LAG, gather_step, 0)
+
+    def merge(sheets):
+        top = sheets[0][0]
+        for sheet in sheets[1:]:
+            top = jnp.maximum(top, sheet[0])
+        total = sum(jnp.exp(sheet[0] - top) for sheet in sheets)
+        return top + jnp.log(total), sum(sheet[1] for sheet in sheets)
+
+    def exchange(level, targets, devices, first):
+        copies = []
+        for n, (target, device) in enumerate(zip(targets, devices)):
+            copy = remote(
+                stats.at[level], target, stat_send.at[first + n], stat_recv.at[first + n], device
+            )
+            copy.start()
+            copies.append(copy)
+        for copy in copies:
+            copy.wait()
+        return merge([stats[level]] + [target[...] for target in targets])
+
+    norm, hit = exchange(0, [from_sibling], [sibling], 0)
+    stats[1, 0], stats[1, 1] = norm, hit
+    norm, hit = exchange(1, [from_z.at[n] for n in range(3)], along_z, 1)
+    stats[2, 0], stats[2, 1] = norm, hit
+    norm, hit = exchange(2, [from_plane.at[n] for n in range(3)], plane, 4)
+    stats[3, 0], stats[3, 1] = norm, norm - hit
+
+    own = stats[3, 1, pl.ds(a * 4 + z, 1), :]
+    loss_ref[...] = jnp.where(c == 0, own[:, :trips], own[:, trips:])
+
+    grad_ref[...] = jnp.zeros_like(grad_ref)
+
+    def gradient_step(quad, unused):
+        scales, targets = [], []
+        for n in range(4):
+            pair = quad * 4 + n
+            in_use, target = read_notes(pair)
+            gap = maxima[pl.ds(pair, 1), :] - stats[3, 0, pl.ds(pair, 1), :]
+            scales.append(jnp.where(in_use, jnp.exp(gap), 0.0))
+            targets.append(target)
+        queries = jnp.concatenate([pair_queries(quad * 4 + n) for n in range(4)], axis=0)
+        for m in range(share // TILE):
+            coefficients = jnp.concatenate(
+                [
+                    (
+                        masses[quad * 4 + n, m * TILE : (m + 1) * TILE, :] * scales[n]
+                        - jnp.where(row_iota == targets[n] - m * TILE, 1.0, 0.0)
+                    ).astype(jnp.bfloat16)
+                    for n in range(4)
+                ],
+                axis=1,
+            )
+            grad_ref[m * TILE : (m + 1) * TILE, :] += jnp.dot(
+                coefficients, queries, preferred_element_type=jnp.float32
+            )
+        return unused
+
+    lax.fori_loop(0, PAIRS // 4, gradient_step, 0)
+
+    def drain(i, unused):
+        s_copy(i, chunk_of(i % 4, i // 4, c)).wait_send()
+        return unused
+
+    lax.fori_loop(0, PAIRS, drain, 0)
+    for j in range(4):
+        if j > 0:
+            z_copy(j, mine).wait_send()
+        x_copy(j, chunk_of(0, j, c)).wait_send()
+        y_copy(j, chunk_of(0, j, c)).wait_send()
+        yd_copy(j, chunk_of(1, j, c)).wait_send()
+        xd_copy(j, chunk_of(2, j, c)).wait_send()
+
+
+def fused_device(
+    entities,
+    relations,
+    candidate_blocks,
+    list_lengths,
+    head_offsets,
+    relation_offsets,
+    target_codes,
+):
+    block_rows, width = entities.shape[1:]
+    trips = target_codes.shape[0]
+    share = block_rows // 4
+    dma = pltpu.SemaphoreType.DMA
+    smem = pl.BlockSpec(memory_space=pltpu.SMEM)
+    vmem = pl.BlockSpec(memory_space=pltpu.VMEM)
+    anywhere = pl.BlockSpec(memory_space=pl.ANY)
+    sheet = (2, PAIRS, 2 * trips)
+    loss, gradient = pl.pallas_call(
+        fused_kernel,
+        out_shape=(
+            jax.ShapeDtypeStruct((1, trips), jnp.float32),
+            jax.ShapeDtypeStruct((share, width), jnp.float32),
+        ),
+        in_specs=[smem, smem, smem, smem, vmem, anywhere, anywhere],
+        out_specs=(vmem, vmem),
+        scratch_shapes=[
+            pltpu.VMEM((block_rows, width), jnp.float32),
+            pltpu.VMEM(relations.shape, jnp.float32),
+            pltpu.VMEM((share, width), jnp.bfloat16),
+            pltpu.VMEM((trips, width), jnp.float32),
+            pltpu.VMEM((trips, width), jnp.int32),
+            pltpu.VMEM((trips, width), jnp.float32),
+            pltpu.VMEM((2 * PAIRS, trips + META, width), jnp.bfloat16),
+            pltpu.VMEM((PAIRS, share, 2 * trips), jnp.float32),
+            pltpu.VMEM((PAIRS, 2 * trips), jnp.float32),
+            pltpu.VMEM((4,) + sheet, jnp.float32),
+            pltpu.VMEM(sheet, jnp.float32),
+            pltpu.VMEM((3,) + sheet, jnp.float32),
+            pltpu.VMEM((3,) + sheet, jnp.float32),
+            dma((LOADS + 1,)),
+            dma((3,)),
+            dma((3,)),
+            dma((4,)),
+            dma((4,)),
+            dma((4,)),
+            dma((4,)),
+            dma((4,)),
+            dma((4,)),
+            dma((4,)),
+            dma((4,)),
+            dma((PAIRS,)),
+            dma((PAIRS,)),
+            dma((7,)),
+            dma((7,)),
+        ],
+        compiler_params=pltpu.CompilerParams(
+            collective_id=0, has_side_effects=True, vmem_limit_bytes=56 * 1024 * 1024
+        ),
+        name="rescal_step",
+    )(
+        candidate_blocks,
+        list_lengths,
+        head_offsets,
+        relation_offsets,
+        target_codes[None],
+        entities,
+        relations,
+    )
+    return (loss.reshape(trips), gradient[None])
+
+
 def solution(mesh):
+    small = mesh.shape["dp"] == 4 and mesh.shape["entity"] == 8
     return jax.shard_map(
-        per_device,
+        fused_device if small else per_device,
         mesh=mesh,
         in_specs=(
             P("entity", None, None),

time: 170 us -> 64 us (0.38)
  Pallas kernels: 0 us -> 59.8 us
  blocking collectives: 56.4 us -> 0 us
  waiting for transfers between devices: 50.6 us -> 0 us
  matrix products: 25.5 us -> 0 us
  between operations: 14.2 us -> 0.64 us
  other arithmetic: 12.3 us -> 0 us
  local copies, waits for them, and re-layouts: 10.1 us -> 3.38 us
    pallas_call x0 -> x1, Pallas kernels: none -> 59.8 us  [fused_device(): pl.pallas_call(fused_kernel, out_shape=(jax.ShapeDtypeStruct((1, trips),...]
    reduce_scatter x1 -> x0, waiting for transfers between devices: 50.6 us -> none  [per_device(): lax.psum_scatter(slot_grads(rounded_table, slot_queries, slot_targets, sl...]
    all_gather x2 -> x0, blocking collectives: 28.4 us -> none  [the longest x1 14.9 us: per_device(): lax.all_gather(query[None], 'entity', axis=0, tiled=True)]
    dot_general x5 -> x0, matrix products: 25.5 us -> none  [the longest x2 14 us: one_step(): lax.dot_general(coefficients, step_queries, (((0,), (0,)), ((), ())), pre...]
    psum x1 -> x0, blocking collectives: 14.1 us -> none  [per_device(): top_mass, top_target = lax.psum((scaled_mass, set_target), 'entity')]
    pmax x1 -> x0, blocking collectives: 13.9 us -> none  [per_device(): lax.pmax(set_max.astype(jnp.bfloat16), 'entity').astype(set_max.dtype)]
    gather x10 -> x0, local copies, waits for them, and re-layouts: 8.85 us -> none  [the longest x1 2.94 us: per_device(): head_rows = jnp.take(table, head_offsets, axis=0)]
    reduce_sum x4 -> x0, other arithmetic: 5.84 us -> none  [the longest x2 5.63 us: one_step(): picked = jnp.sum(jnp.where(is_target, scores, 0.0), axis=1)]
  transfers between devices with their start and end apart: 1 -> 0, of which waited for: 1 -> 0; matrix products, arithmetic and copies ran while one was open for 0% -> 0% of each run, Pallas kernels for 0% -> 0%
where the time goes in v1:
time: 64 us; the launch traced here: 63.8 us
  Pallas kernels  59.8 us (93%)
  local copies, waits for them, and re-layouts  3.38 us (5%)
  between operations  0.64 us (1%)
    pallas_call x1, Pallas kernels, fused_device(): pl.pallas_call(fused_kernel, out_shape=(jax.ShapeDtypeStruct((1, trips),...  59.8 us
    unnamed x2, local copies, waits for them, and re-layouts  3.38 us

profile of v1, /device:TPU:0, one launch (start us, length us, event | category | flops | bytes accessed | tf_op | source)
XLA Modules:
  0.0 63.8 jit_solution(6691141816929981799)
XLA Ops:
  0.6 59.8 %rescal_step.1 = (f32[1,128]{1,0:T(1,128)}, f32[1024,256]{1,0:T(8,128)}) custom-call(s32[8,8]{1,0:T(8,128)} %lists_ref.1, s32[1,8]{1,0:T(1,128)} %lengths_ref.1, s32[128]{0:T(128)} %heads_ref.1, s32[128]{0:T(128)} %kinds_ref.1, s32[1,128]{1,0:T(1,128)} %bitcast.4, f32[1,4096,256]{2,1,0:T(8,128)} %table_hbm.1, f32[32,256,256]{2,1,0:T(8,128)} %relations_hbm.1), custom_call_target="tpu_custom_call" | custom-call | tf_op jit(solution)/shard_map/rescal_step/pallas_call | solution.py:506
  60.4 1.1 %copy.11 = f32[128]{0:T(128)} copy(f32[128]{0:T(128)} %bitcast.5) | data formatting | bytes 1024
  61.5 2.3 %copy.12 = f32[1,1024,256]{2,1,0:T(8,128)} copy(f32[1,1024,256]{2,1,0:T(8,128)} %bitcast.3) | data formatting | bytes 2097152
